TPU v7x, 512 devices: a whole 4x4x16 slice. The times are simulated.
512 devices in a mesh: hist: 64 (over z_lo, x, y), dom: 8 (over z_hi, core).
Axes of the slice: x: 4, y: 4, z: 16 (z_hi: 4, z_lo: 4; z = z_hi * 4 + z_lo), core: 2. Of those that a mesh axis runs over, the one named last changes fastest.
Arguments:
- coords: float32 [6, 1048576], P(None, ('dom', 'hist')), may hold values from -3 to 3
- charge: float32 [1048576], P(('dom', 'hist')), may hold values from 0.02 to 0.2
- row_index: int32 [1048576], P(('dom', 'hist')), may hold values from 0 to 511, as said below
- block_col: int32 [8192], P(('dom', 'hist')), may hold values from 0 to 496
- col_offset: int32 [1048576], P(('dom', 'hist')), may hold values from 0 to 15
- transfer_map: float32 [6, 84], replicated
- history: bfloat16 [512, 2, 512, 512], P('hist', None, 'dom'), may hold values from -16 to 16
- retard_index: int32 [512], P('hist'), may hold values from 0 to 16
- retard_frac: float32 [512], P('hist'), may hold values from 0 to 1
- retard_weight: float32 [512], P('hist'), may hold values from 0.005 to 0.05
- z_kernel: float32 [512, 512], P(None, 'dom')
- x_kernel: float32 [512, 512], replicated
Outputs:
- kicked: float32 [6, 1048576], P(None, ('dom', 'hist'))
- field: float32 [2, 512, 512], P(None, 'dom', 'hist')
- deposit: float32 [2, 512, 512], P(None, 'dom', 'hist')
Inputs may be any that keep to these rules, and one draw needn't show every extreme that they name: `row_index`: particle i lies in grid slab i // (1048576 // 8): its row is that slab's number times 64 plus 0 to 63.
All inputs are finite; a program needn't handle non-finite values.
Results may differ from a plain program's by a relative error of at most 0.0019.
Values may be sent and summed in bfloat16 or wider, within the bound.
A program may use at most 64 MiB of HBM per device.

v0:
```python
import jax
import jax.numpy as jnp
from jax import lax
from jax.sharding import PartitionSpec as P


def monomials(coords):
    products = [jnp.ones_like(coords[0])]
    for first in range(6):
        products.append(coords[first])
    for first in range(6):
        for second in range(first, 6):
            products.append(coords[first] * coords[second])
    for first in range(6):
        for second in range(first, 6):
            for third in range(second, 6):
                products.append(coords[first] * coords[second] * coords[third])
    return jnp.stack(products)


def retarded_source(history, retard_index, retard_frac, retard_weight):
    count_steps, comps, rows_here, width = history.shape

    def add_step(position, total):
        frame = lax.dynamic_index_in_dim(history, position, 0, keepdims=False).astype(jnp.float32)
        padded = jnp.pad(frame, ((0, 0), (0, 0), (width + 1, 0)))
        lag = retard_index[position]
        near = lax.dynamic_slice_in_dim(padded, width + 1 - lag, width, 2)
        far = lax.dynamic_slice_in_dim(padded, width - lag, width, 2)
        fraction = retard_frac[position]
        return total + retard_weight[position] * ((1.0 - fraction) * near + fraction * far)

    start = jnp.zeros((comps, rows_here, width), jnp.float32)
    return lax.fori_loop(0, count_steps, add_step, start)


def local(
    coords,
    charge,
    row_index,
    block_col,
    col_offset,
    transfer_map,
    history,
    retard_index,
    retard_frac,
    retard_weight,
    z_kernel,
    x_kernel,
):
    highest = lax.Precision.HIGHEST
    slab_rows = history.shape[2]
    width = history.shape[3]
    strip_width = width // lax.axis_size("hist")
    particles = coords.shape[1]
    group_size = min(1024, particles)
    count_groups = particles // group_size
    block_size = particles // block_col.shape[0]
    slab_start = lax.axis_index("dom") * slab_rows
    source = retarded_source(history, retard_index, retard_frac, retard_weight)
    spread = jnp.einsum("crx,xy->cry", source, x_kernel, precision=highest)
    partial_field = jnp.einsum("rs,csy->cry", z_kernel, spread, precision=highest)
    total_field = lax.psum(partial_field, ("hist", "dom"))
    slab_field = lax.dynamic_slice_in_dim(total_field, slab_start, slab_rows, 1)
    field_out = lax.dynamic_slice_in_dim(
        slab_field, lax.axis_index("hist") * strip_width, strip_width, 2
    )
    slab_rounded = slab_field.astype(jnp.bfloat16)
    folded = jnp.transpose(slab_rounded, (1, 0, 2)).reshape(slab_rows, 2 * width)
    pushed = jnp.dot(transfer_map, monomials(coords), precision=highest)
    column = jnp.repeat(block_col, block_size) + col_offset
    local_row = row_index - slab_start
    weight_pair = jnp.stack([charge, charge * pushed[1]]).astype(jnp.bfloat16)
    row_groups = local_row.reshape(count_groups, group_size)
    column_groups = column.reshape(count_groups, group_size)
    weight_groups = jnp.transpose(weight_pair.reshape(2, count_groups, group_size), (1, 0, 2))
    row_iota = lax.iota(jnp.int32, slab_rows)
    column_iota = lax.iota(jnp.int32, width)

    def one_group(accumulated, pieces):
        group_rows, group_columns, group_weights = pieces
        row_hot = (row_iota[:, None] == group_rows[None, :]).astype(jnp.bfloat16)
        column_hot = (group_columns[:, None] == column_iota[None, :]).astype(jnp.bfloat16)
        weighted = jnp.concatenate(
            [group_weights[0][:, None] * column_hot, group_weights[1][:, None] * column_hot], axis=1
        )
        accumulated = accumulated + jnp.dot(row_hot, weighted, preferred_element_type=jnp.float32)
        sampled_rows = lax.dot_general(
            row_hot, folded, (((0,), (0,)), ((), ())), preferred_element_type=jnp.float32
        )
        column_mask = column_hot.astype(jnp.float32)
        longitudinal = jnp.sum(sampled_rows[:, :width] * column_mask, axis=1)
        transverse = jnp.sum(sampled_rows[:, width:] * column_mask, axis=1)
        return (accumulated, jnp.stack([longitudinal, transverse]))

    empty = jnp.zeros((slab_rows, 2 * width), jnp.float32)
    deposit_local, sampled_groups = lax.scan(
        one_group, empty, (row_groups, column_groups, weight_groups)
    )
    sampled = jnp.transpose(sampled_groups, (1, 0, 2)).reshape(2, particles)
    deposit_split = lax.psum_scatter(
        deposit_local.reshape(slab_rows, 2, width), "hist", scatter_dimension=2, tiled=True
    )
    deposit_out = jnp.transpose(deposit_split, (1, 0, 2))
    kicked = pushed.at[5].add(0.5 * sampled[0]).at[1].add(0.5 * sampled[1])
    return (kicked, field_out, deposit_out)


def solution(mesh):
    return jax.shard_map(
        local,
        mesh=mesh,
        in_specs=(
            P(None, ("dom", "hist")),
            P(("dom", "hist")),
            P(("dom", "hist")),
            P(("dom", "hist")),
            P(("dom", "hist")),
            P(),
            P("hist", None, "dom", None),
            P("hist"),
            P("hist"),
            P("hist"),
            P(None, "dom"),
            P(),
        ),
        out_specs=(P(None, ("dom", "hist")), P(None, "dom", "hist"), P(None, "dom", "hist")),
        check_vma=False,
    )
```

profile of v0, /device:TPU:128, one launch (start us, length us, event | category | flops | bytes accessed | tf_op | source)
XLA Modules:
  0.0 956.1 jit_solution(17558240199381335158)
XLA Ops:
  7.2 76.3 %while.31 = (s32[]{:T(128)}, f32[2,64,512]{2,1,0:T(8,128)S(1)}, f32[8]{0:T(128)}, f32[8]{0:T(128)}, bf16[8,2,64,512]{3,2,1,0:T(8,128)(2,1)}, /*index=5*/s32[8]{0...) while((s32[]{:T(128)}, f32[2,64,512]{2,1,0:T(8,128)S(1)}, ...), condition=%wide.region_1.2_spmd.clone, body=%wide.region_0.1_spmd.clone.sunk | while | flops 524428 | bytes 1966899 | solution.py:34
  7.3 1.3 dynamic_slice.109
  8.6 1.3 dynamic_slice.108
  15.4 1.5 select_add_fusion.2
  18.1 1.3 dynamic_slice.108
  24.9 1.5 select_add_fusion.2
  27.6 1.3 dynamic_slice.108
  34.4 1.5 select_add_fusion.2
  37.2 1.3 dynamic_slice.108
  43.9 1.5 select_add_fusion.2
  45.4 1.2 dynamic_slice.109
  46.7 1.3 dynamic_slice.108
  53.5 1.5 select_add_fusion.2
  56.2 1.3 dynamic_slice.108
  63.0 1.5 select_add_fusion.2
  65.7 1.3 dynamic_slice.108
  72.5 1.5 select_add_fusion.2
  75.3 1.3 dynamic_slice.108
  82.0 1.5 select_add_fusion.2
  84.3 3.2 convolution_bitcast_fusion
  90.0 472.6 %all-reduce.3.cloned.1.call-done = f32[2,512,512]{1,2,0:T(8,128)} async-done(((f32[2,512,512]{1,2,0:T(8,128)}), f32[2,512,512]{1,2,0:T(8,128)}) %all-reduce.3.cloned.1.call-update) | async-done | bytes 2097168 | tf_op jit(solution)/shard_map/psum | solution.py:63
  564.0 5.3 while.32
  570.8 1.5 constant_dynamic-slice_fusion.2
  572.3 377.0 %reduce-scatter.2.cloned.1.call-done = f32[64,2,8]{0,2,1:T(8,128)} async-done(((f32[64,2,512]{0,2,1:T(8,128)}), f32[64,2,8]{0,2,1:T(8,128)}) %reduce-scatter.2.cloned.1.call-update) | async-done | bytes 4112 | tf_op jit(solution)/shard_map/reduce_scatter | solution.py:101
  (98 shorter events, 36.8 us)
Async XLA Ops:
  7.2 76.4 %copy-start = (f32[512,512]{1,0:T(8,128)S(1)}, f32[512,512]{1,0:T(8,128)}, u32[]{:S(2)}) copy-start(f32[512,512]{1,0:T(8,128)} %param.31) | copy-start | bytes 3145732
  7.2 555.5 %all-reduce.3.cloned.1.call-start = ((), (), s32[]{:S(2)}) async-start(), calls=%async_computation.1 | async-start | bytes 4194304 | tf_op jit(solution)/shard_map/psum | solution.py:63
  7.2 77.0 %copy-start.2 = (f32[512,64]{0,1:T(8,128)S(1)}, f32[512,64]{0,1:T(8,128)}, u32[]{:S(2)}) copy-start(f32[512,64]{0,1:T(8,128)} %param.30) | copy-start | bytes 393220
  84.3 3.3 copy-start.1
  84.3 3.5 copy-start.5
  84.3 3.5 copy-start.8
  87.5 0.7 copy-start.6
  87.5 1.9 copy-start.7
  87.5 2.4 copy-start.4
  87.5 861.8 %reduce-scatter.2.cloned.1.call-start = ((), (), s32[]{:S(2)}) async-start(), calls=%async_computation.2 | async-start | bytes 532480 | tf_op jit(solution)/shard_map/reduce_scatter | solution.py:101
  570.8 378.5 %copy-start.3 = (f32[6,2048]{1,0:T(8,128)}, f32[6,2048]{1,0:T(8,128)S(1)}, u32[]{:S(2)}) copy-start(f32[6,2048]{1,0:T(8,128)S(1)} %scatter-add.9) | copy-start | bytes 147460
Sparse Core Ops, SparseCore 0:
  87.6 474.9 all-reduce.2
  570.5 378.7 reduce-scatter.1
where the time goes:
time: 957 us; the launch traced here: 956 us
  waiting for transfers between devices  850 us (89%)
  local copies, waits for them, and re-layouts  43 us (4%)
  loops' own time  26.3 us (3%)
  other arithmetic  15.2 us (2%)
  between operations  14.3 us (1%)
    psum x1, waiting for transfers between devices, local(): total_field = lax.psum(partial_field, ('hist', 'dom'))  473 us
    reduce_scatter x1, waiting for transfers between devices, local(): lax.psum_scatter(deposit_local.reshape(slab_rows, 2, width), 'hist', scat...  377 us
    another operation x1, loops' own time, retarded_source(): return lax.fori_loop(0, count_steps, add_step, start)  26.2 us
  transfers between devices with their start and end apart: 2, of which 2 were waited for; matrix products, arithmetic and copies ran while one was open for 0% of the time, Pallas kernels for 0%

commit v1 on v0

--- a/solution.py
+++ b/solution.py
@@ -60,7 +60,9 @@
     source = retarded_source(history, retard_index, retard_frac, retard_weight)
     spread = jnp.einsum("crx,xy->cry", source, x_kernel, precision=highest)
     partial_field = jnp.einsum("rs,csy->cry", z_kernel, spread, precision=highest)
-    total_field = lax.psum(partial_field, ("hist", "dom"))
+    total_field = partial_field
+    for tick in ("hist", "dom"):
+        total_field = jax.lax.psum(total_field, axis_name=tick)
     slab_field = lax.dynamic_slice_in_dim(total_field, slab_start, slab_rows, 1)
     field_out = lax.dynamic_slice_in_dim(
         slab_field, lax.axis_index("hist") * strip_width, strip_width, 2

time: 957 us -> 1350 us (1.41)
  waiting for transfers between devices: 850 us -> 1240 us
    psum x1 -> x2, waiting for transfers between devices: 473 us -> 860 us  [local(): total_field = jax.lax.psum(total_field, axis_name=tick)]
  transfers between devices with their start and end apart: 2 -> 3, of which waited for: 2 -> 3; matrix products, arithmetic and copies ran while one was open for 0% -> 0% of each run, Pallas kernels for 0% -> 0%
where the time goes in v1:
time: 1350 us
  waiting for transfers between devices  1240 us (92%)
  local copies, waits for them, and re-layouts  42.9 us (3%)
  loops' own time  26.3 us (2%)
  other arithmetic  15.3 us (1%)
  between operations  14.1 us (1%)
    psum x2, waiting for transfers between devices, local(): total_field = jax.lax.psum(total_field, axis_name=tick)  860 us
    reduce_scatter x1, waiting for transfers between devices, local(): lax.psum_scatter(deposit_local.reshape(slab_rows, 2, width), 'hist', scat...  379 us
  transfers between devices with their start and end apart: 3, of which 3 were waited for; matrix products, arithmetic and copies ran while one was open for 0% of the time, Pallas kernels for 0%

profile of v1, /device:TPU:128, one launch (start us, length us, event | category | flops | bytes accessed | tf_op | source)
XLA Modules:
  0.0 1345.3 jit_solution(13961173424506040685)
XLA Ops:
  7.2 76.3 %while.31 = (s32[]{:T(128)}, f32[2,64,512]{2,1,0:T(8,128)S(1)}, f32[8]{0:T(128)}, f32[8]{0:T(128)}, bf16[8,2,64,512]{3,2,1,0:T(8,128)(2,1)}, /*index=5*/s32[8]{0...) while((s32[]{:T(128)}, f32[2,64,512]{2,1,0:T(8,128)S(1)}, ...), condition=%wide.region_1.2_spmd.clone, body=%wide.region_0.1_spmd.clone.sunk | while | flops 524428 | bytes 1966899 | solution.py:34
  7.3 1.3 dynamic_slice.109
  8.6 1.3 dynamic_slice.108
  15.4 1.5 select_add_fusion.2
  18.1 1.3 dynamic_slice.108
  24.9 1.5 select_add_fusion.2
  27.6 1.3 dynamic_slice.108
  34.4 1.5 select_add_fusion.2
  37.2 1.3 dynamic_slice.108
  43.9 1.5 select_add_fusion.2
  46.7 1.3 dynamic_slice.108
  53.5 1.5 select_add_fusion.2
  56.2 1.3 dynamic_slice.108
  63.0 1.5 select_add_fusion.2
  65.7 1.3 dynamic_slice.108
  72.5 1.5 select_add_fusion.2
  75.3 1.3 dynamic_slice.108
  82.0 1.5 select_add_fusion.2
  84.3 3.2 convolution_bitcast_fusion
  87.8 729.1 %all-reduce.4.cloned.1.call-done = f32[2,512,512]{1,2,0:T(8,128)} async-done(((f32[2,512,512]{1,2,0:T(8,128)}), f32[2,512,512]{1,2,0:T(8,128)}) %all-reduce.4.cloned.1.call-update) | async-done | bytes 2097168 | tf_op jit(solution)/shard_map/psum | solution.py:65
  819.1 131.3 %all-reduce.6.cloned.1.call-done = f32[2,512,512]{1,2,0:T(8,128)} async-done(((f32[2,512,512]{1,2,0:T(8,128)}), f32[2,512,512]{1,2,0:T(8,128)}) %all-reduce.6.cloned.1.call-update) | async-done | bytes 2097168 | tf_op jit(solution)/shard_map/psum | solution.py:65
  951.7 5.3 while.32
  958.6 1.5 constant_dynamic-slice_fusion.2
  960.1 378.7 %reduce-scatter.2.cloned.1.call-done = f32[64,2,8]{0,2,1:T(8,128)} async-done(((f32[64,2,512]{0,2,1:T(8,128)}), f32[64,2,8]{0,2,1:T(8,128)}) %reduce-scatter.2.cloned.1.call-update) | async-done | bytes 4112 | tf_op jit(solution)/shard_map/reduce_scatter | solution.py:103
  (101 shorter events, 38.0 us)
Async XLA Ops:
  7.2 76.4 %copy-start = (f32[512,512]{1,0:T(8,128)S(1)}, f32[512,512]{1,0:T(8,128)}, u32[]{:S(2)}) copy-start(f32[512,512]{1,0:T(8,128)} %param.31) | copy-start | bytes 3145732
  7.2 809.8 %all-reduce.4.cloned.1.call-start = ((), (), s32[]{:S(2)}) async-start(), calls=%async_computation.1 | async-start | bytes 4194304 | tf_op jit(solution)/shard_map/psum | solution.py:65
  7.2 77.0 %copy-start.2 = (f32[512,64]{0,1:T(8,128)S(1)}, f32[512,64]{0,1:T(8,128)}, u32[]{:S(2)}) copy-start(f32[512,64]{0,1:T(8,128)} %param.30) | copy-start | bytes 393220
  84.3 3.3 copy-start.5
  84.3 3.3 copy-start.1
  87.5 729.6 %copy-start.6 = (s32[2048]{0:T(1024)S(1)}, s32[2048]{0:T(1024)}, u32[]{:S(2)}) copy-start(s32[2048]{0:T(1024)} %param.24) | copy-start | bytes 24580
  87.5 729.6 %copy-start.8 = (s32[16]{0:T(128)S(1)}, s32[16]{0:T(128)}, u32[]{:S(2)}) copy-start(s32[16]{0:T(128)} %param.23) | copy-start | bytes 196
  87.5 863.0 %all-reduce.6.cloned.1.call-start = ((), (), s32[]{:S(2)}) async-start(), calls=%async_computation.2 | async-start | bytes 4194304 | tf_op jit(solution)/shard_map/psum | solution.py:65
  817.0 1.5 copy-start.7
  817.0 2.0 copy-start.4
  817.0 521.8 %reduce-scatter.2.cloned.1.call-start = ((), (), s32[]{:S(2)}) async-start(), calls=%async_computation.3 | async-start | bytes 532480 | tf_op jit(solution)/shard_map/reduce_scatter | solution.py:103
  958.6 380.1 %copy-start.3 = (f32[6,2048]{1,0:T(8,128)}, f32[6,2048]{1,0:T(8,128)S(1)}, u32[]{:S(2)}) copy-start(f32[6,2048]{1,0:T(8,128)S(1)} %scatter-add.9) | copy-start | bytes 147460
Sparse Core Ops, SparseCore 0:
  87.6 729.3 all-reduce.3
  820.2 130.2 all-reduce.5
  958.3 380.4 reduce-scatter.1
